TPU v7x, 512 devices: a whole 4x8x8 slice. The times are simulated.
512 devices in a mesh: seq: 32 (over x_hi, y, core), batch: 16 (over z, x_lo).
Axes of the slice: x: 4 (x_hi: 2, x_lo: 2; x = x_hi * 2 + x_lo), y: 8, z: 8, core: 2. Of those that a mesh axis runs over, the one named last changes fastest.
Arguments:
- inputs: bfloat16 [16, 32768, 512], P('batch', 'seq'), may hold values from -6 to 6
- gates: bfloat16 [16, 32768, 512], P('batch', 'seq'), may hold values from 0.099609375 to 2
- cotangent: bfloat16 [16, 32768, 512], P('batch', 'seq'), may hold values from -6 to 6
- first_factor: bfloat16 [128, 256, 256], P('seq'), may hold values from -0.375 to 0.375
- second_factor: bfloat16 [256, 128, 128], P('seq'), may hold values from -0.5 to 0.5
Outputs:
- input_grad: bfloat16 [16, 32768, 512], P('batch', 'seq')
- first_grad: float32 [128, 256, 256], P('seq', 'batch')
- second_grad: float32 [256, 128, 128], P('seq', 'batch')
All inputs are finite; a program needn't handle non-finite values.
Results may differ from a plain program's by a relative error of at most 0.0057.
Values may be sent and summed in bfloat16 or wider, within the bound.
No kernel may reach another device: no remote copies, remote signals or barrier semaphores. Data moves between devices by JAX's collectives and lax.ppermute only.
A program may use at most 64 MiB of HBM per device.

v0:
```python
import jax
import jax.numpy as jnp
from jax import lax
from jax.sharding import PartitionSpec as P


def per_device(inputs, gates, cotangent, first_factor, second_factor):
    count = inputs.shape[0]
    channels = inputs.shape[2]
    blocks_here = first_factor.shape[0]
    width_q = first_factor.shape[1]
    rows_here = second_factor.shape[0]
    width_p = second_factor.shape[1]
    source = inputs.reshape(count, blocks_here, width_q, channels)
    scaled = (cotangent.astype(jnp.float32) * gates.astype(jnp.float32)).astype(jnp.bfloat16)
    scaled = scaled.reshape(count, rows_here, width_p, channels)
    mixed = jnp.einsum(
        "pij,spjc->spic", first_factor, source, preferred_element_type=jnp.float32
    ).astype(jnp.bfloat16)
    back = jnp.einsum(
        "qkp,sqkc->sqpc", second_factor, scaled, preferred_element_type=jnp.float32
    ).astype(jnp.bfloat16)
    spread = lax.all_to_all(mixed, "seq", split_axis=2, concat_axis=1, tiled=True)
    returned = lax.all_to_all(back, "seq", split_axis=2, concat_axis=1, tiled=True)
    second_local = jnp.einsum("sqkc,spqc->qkp", scaled, spread, preferred_element_type=jnp.float32)
    input_grad = jnp.einsum(
        "pij,sipc->spjc", first_factor, returned, preferred_element_type=jnp.float32
    )
    input_grad = input_grad.astype(jnp.bfloat16).reshape(count, blocks_here * width_q, channels)
    first_local = jnp.einsum("sipc,spjc->pij", returned, source, preferred_element_type=jnp.float32)
    parts = lax.axis_size("batch")
    total = count * parts
    first_sum, second_sum = lax.psum((first_local, second_local), "batch")
    position = lax.axis_index("batch")
    first_grad = lax.dynamic_slice_in_dim(
        first_sum, position * (width_q // parts), width_q // parts, 1
    )
    second_grad = lax.dynamic_slice_in_dim(
        second_sum, position * (width_p // parts), width_p // parts, 1
    )
    return (input_grad, first_grad / total, second_grad / total)


def solution(mesh):
    in_specs = (
        P("batch", "seq", None),
        P("batch", "seq", None),
        P("batch", "seq", None),
        P("seq", None, None),
        P("seq", None, None),
    )
    out_specs = (P("batch", "seq", None), P("seq", "batch", None), P("seq", "batch", None))
    return jax.shard_map(
        per_device, mesh=mesh, in_specs=in_specs, out_specs=out_specs, check_vma=False
    )
```

profile of v0, /device:TPU:6, one launch (start us, length us, event | category | flops | bytes accessed | tf_op | source)
XLA Modules:
  0.0 245.3 jit_solution(3019127348043703428)
XLA Ops:
  7.2 0.0 copy-start
  7.2 1.2 copy-done
  8.4 1.6 fusion.1
  10.0 1.8 copy.25
  11.8 10.2 %all-to-all-start.1 = ((bf16[1,4,256,512]{3,1,0,2:T(4,128)(2,1)}), bf16[1,4,256,512]{3,1,0,2:T(4,128)(2,1)S(1)}, u32[]{:S(2)}, u32[]{:S(2)}) async-start(bf16[1,4,256,512]{3,1,0,2:T(4,128)(2,1)} %copy.25), calls=%async_computation.1 | async-start | bytes 2097152 | tf_op jit(solution)/shard_map/all_to_all | solution.py:23
  22.0 0.0 copy-start.3
  22.0 1.9 multiply_convert_fusion
  23.9 0.0 copy-done.3
  23.9 1.5 fusion
  25.4 2.7 %copy.21 = bf16[1,8,128,512]{3,1,0,2:T(8,128)(2,1)} copy(bf16[1,8,128,512]{2,3,1,0:T(8,128)(2,1)} %fusion) | data formatting | bytes 2097152 | tf_op jit(solution)/shard_map/convert_element_type | solution.py:22
  28.1 21.2 %all-to-all-done.1 = bf16[1,4,256,512]{3,1,0,2:T(4,128)(2,1)S(1)} async-done(((bf16[1,4,256,512]{3,1,0,2:T(4,128)(2,1)}), bf16[1,4,256,512]{3,1,0,2:T(4,128)(2,1)S(1)}, u32[]{:S(2)}, u32[]{:S(2)}) %all-to-all-start.1) | async-done | bytes 1048608 | tf_op jit(solution)/shard_map/all_to_all | solution.py:23
  49.3 0.0 copy-start.1
  49.3 1.0 copy-done.1
  50.2 6.7 %all-to-all-start = ((bf16[1,8,128,512]{3,1,0,2:T(8,128)(2,1)}), bf16[1,8,128,512]{3,1,0,2:T(8,128)(2,1)S(1)}, u32[]{:S(2)}, u32[]{:S(2)}) async-start(bf16[1,8,128,512]{3,1,0,2:T(8,128)(2,1)} %copy.21), calls=%async_computation | async-start | bytes 2097152 | tf_op jit(solution)/shard_map/all_to_all | solution.py:24
  56.9 0.0 all-reduce.3.cloned.1.call-start
  57.0 1.4 copy.40
  58.4 1.8 copy.27
  60.2 2.2 reshape.43
  62.4 2.5 %fusion.7 = f32[8,128,128]{2,1,0:T(8,128)} fusion(bf16[8,128,512]{2,1,0:T(8,128)(2,1)S(1)} %bitcast.43, bf16[128,8,512]{2,0,1:T(8,128)(2,1)} %reshape.43), kind=kOutput, calls=%fused_computation.14 | convolution fusion | flops 134217728 | bytes 2621440 | tf_op jit(solution)/shard_map/sqkc,spqc->qkp/dot_general | solution.py:25
  64.8 19.4 %all-to-all-done = bf16[1,8,128,512]{3,1,0,2:T(8,128)(2,1)S(1)} async-done(((bf16[1,8,128,512]{3,1,0,2:T(8,128)(2,1)}), bf16[1,8,128,512]{3,1,0,2:T(8,128)(2,1)S(1)}, u32[]{:S(2)}, u32[]{:S(2)}) %all-to-all-start) | async-done | bytes 1048608 | tf_op jit(solution)/shard_map/all_to_all | solution.py:24
  84.2 1.5 fusion.2
  85.7 0.0 copy-start.2
  85.7 0.0 all-reduce.3.cloned.1.call-update
  85.7 1.0 copy-done.2
  86.7 1.5 convolution_convert_fusion.2
  88.2 147.5 %all-reduce.3.cloned.1.call-done = (f32[4,256,256]{2,1,0:T(8,128)}, f32[8,128,128]{2,1,0:T(8,128)}) async-done(((f32[4,256,256]{2,1,0:T(8,128)}, f32[8,128,128]{2,1,0:T(8,128)}), (f32[4,256,256]{2,1,0:T(8,128)}, f32[8,128,128]{2,1,0:T(8,128)})) %all-reduce.3.cloned.1.call-update) | async-done | bytes 1572880 | tf_op jit(solution)/shard_map/psum | solution.py:33
  235.6 1.5 dynamic-slice_multiply_fusion
  237.1 1.4 dynamic-slice_multiply_fusion.1
Async XLA Ops:
  7.2 1.2 copy-start
  11.8 37.5 %all-to-all-start.1 = ((bf16[1,4,256,512]{3,1,0,2:T(4,128)(2,1)}), bf16[1,4,256,512]{3,1,0,2:T(4,128)(2,1)S(1)}, u32[]{:S(2)}, u32[]{:S(2)}) async-start(bf16[1,4,256,512]{3,1,0,2:T(4,128)(2,1)} %copy.25), calls=%async_computation.1 | async-start | bytes 2097152 | tf_op jit(solution)/shard_map/all_to_all | solution.py:23
  22.0 1.9 copy-start.3
  49.3 1.0 copy-start.1
  50.2 33.9 %all-to-all-start = ((bf16[1,8,128,512]{3,1,0,2:T(8,128)(2,1)}), bf16[1,8,128,512]{3,1,0,2:T(8,128)(2,1)S(1)}, u32[]{:S(2)}, u32[]{:S(2)}) async-start(bf16[1,8,128,512]{3,1,0,2:T(8,128)(2,1)} %copy.21), calls=%async_computation | async-start | bytes 2097152 | tf_op jit(solution)/shard_map/all_to_all | solution.py:24
  56.9 178.7 %all-reduce.3.cloned.1.call-start = ((), (), s32[]{:S(2)}) async-start(), calls=%async_computation.2 | async-start | bytes 3145728 | tf_op jit(solution)/shard_map/psum | solution.py:33
  85.7 1.0 copy-start.2
Sparse Core Ops, SparseCore 0:
  85.8 149.7 all-reduce.2
where the time goes:
time: 246 us; the launch traced here: 245 us
  waiting for transfers between devices  188 us (76%)
  starting transfers between devices  17 us (7%)
  between operations  14.1 us (6%)
  local copies, waits for them, and re-layouts  13.1 us (5%)
  matrix products  8.46 us (3%)
  other arithmetic  4.72 us (2%)
    psum x1, waiting for transfers between devices, per_device(): first_sum, second_sum = lax.psum((first_local, second_local), 'batch')  147 us
    all_to_all x1, waiting for transfers between devices, per_device(): lax.all_to_all(mixed, 'seq', split_axis=2, concat_axis=1, tiled=True)  21.2 us
    all_to_all x1, waiting for transfers between devices, per_device(): lax.all_to_all(back, 'seq', split_axis=2, concat_axis=1, tiled=True)  19.4 us
    all_to_all x1, starting transfers between devices, per_device(): lax.all_to_all(mixed, 'seq', split_axis=2, concat_axis=1, tiled=True)  10.2 us
    all_to_all x1, starting transfers between devices, per_device(): lax.all_to_all(back, 'seq', split_axis=2, concat_axis=1, tiled=True)  6.68 us
  transfers between devices with their start and end apart: 3, of which 3 were waited for; matrix products, arithmetic and copies ran while one was open for 6% of the time, Pallas kernels for 0%

commit v1 on v0

v1 whole, which is shorter than its diff:
```python
import jax
import jax.numpy as jnp
from jax import lax
from jax.experimental import pallas as pl
from jax.experimental.pallas import tpu as pltpu
from jax.sharding import PartitionSpec as P

F32 = jnp.float32
BF16 = jnp.bfloat16
CHUNK = 256
LANES = 128
MIB = 1024 * 1024


def dot(a, b, contract_a, contract_b):
    return lax.dot_general(a, b, (((contract_a,), (contract_b,)), ((), ())), preferred_element_type=F32)


def product(cotangent, gates):
    return (cotangent.astype(F32) * gates.astype(F32)).astype(BF16)


def send_kernel(inputs, gates, cotangent, first, second, send, spread):
    rows, width_p, _ = second.shape
    blocks, width_q, _ = first.shape
    owners, lines, chunk = send.shape
    lines //= 2
    for q in range(rows):
        part = pl.ds(q * width_p, width_p)
        back = dot(second[q], product(cotangent[0, part, :], gates[0, part, :]), 0, 0)
        for lane in range(spread.shape[0]):
            spread[lane, pl.ds(q, width_p, stride=rows), :] = back[:, lane * LANES:(lane + 1) * LANES]
    for lane in range(spread.shape[0]):
        send[:, :lines, lane * LANES:(lane + 1) * LANES] = (
            spread[lane].reshape(owners, lines, LANES).astype(BF16)
        )
    parts = []
    for p in range(blocks):
        mixed = dot(first[p], inputs[0, p * width_q:(p + 1) * width_q, :], 1, 0)
        parts.append(mixed.reshape(owners, rows, chunk))
    send[:, lines:, :] = jnp.concatenate(parts, axis=1).astype(BF16)


def grads_kernel(got, inputs, gates, cotangent, out, spread):
    owners, lines, channels = got.shape
    lines //= 2
    shares, height, width_q = out.shape
    width_p = LANES
    rows = gates.shape[1] // width_p
    blocks = inputs.shape[1] // width_q
    wide = got[:, :lines, :].astype(F32).reshape(owners, blocks, rows, channels)
    parts = []
    for p in range(blocks):
        back = wide[:, p].reshape(width_q, channels).astype(BF16)
        grad = dot(back, inputs[0, p * width_q:(p + 1) * width_q, :], 1, 1)
        parts.append(grad.reshape(shares, width_q // shares, width_q))
    for lane in range(spread.shape[0]):
        spread[lane] = (
            got[:, lines:, lane * LANES:(lane + 1) * LANES].astype(F32).reshape(owners * lines, LANES)
        )
    seconds = []
    for q in range(rows):
        mixed = jnp.concatenate(
            [spread[lane, pl.ds(q, width_p, stride=rows), :] for lane in range(spread.shape[0])], axis=1
        ).astype(BF16)
        part = pl.ds(q * width_p, width_p)
        grad = dot(product(cotangent[0, part, :], gates[0, part, :]), mixed, 1, 1)
        seconds.append(grad.reshape(shares, width_p // shares, width_p))
    half = rows // 2
    for q in range(half):
        parts.append(jnp.concatenate([seconds[q], seconds[q + half]], axis=2))
    out[...] = jnp.concatenate(parts, axis=1).astype(BF16)


def input_kernel(got, factor, out):
    blocks, width, _ = factor.shape
    owners, lines, channels = got.shape
    wide = got[:, :lines // 2, :].astype(F32).reshape(owners, blocks, width // owners, channels)
    for p in range(blocks):
        back = wide[:, p].reshape(width, channels).astype(BF16)
        out[0, p * width:(p + 1) * width, :] = dot(factor[p], back, 0, 0).astype(BF16)


def sum_kernel(got, first, second):
    shares = got.shape[0]
    blocks, height, width_q = first.shape
    rows, depth, width_p = second.shape
    total = got[0].astype(F32)
    for share in range(1, shares):
        total = total + got[share].astype(F32)
    total = total * (1.0 / shares)
    cut = blocks * height
    first[...] = total[:cut].reshape(first.shape)
    half = rows // 2
    second[:half] = total[cut:, :width_p].reshape(half, depth, width_p)
    second[half:] = total[cut:, width_p:].reshape(half, depth, width_p)


def whole(shape):
    return pl.BlockSpec(shape, lambda i: (0,) * len(shape))


def sliced(shape):
    return pl.BlockSpec(shape[:-1] + (CHUNK,), lambda i: (0,) * (len(shape) - 1) + (i,))


def near(count):
    return [pl.BlockSpec(memory_space=pltpu.VMEM)] * count


def cost(flops, bytes_accessed):
    return pl.CostEstimate(flops=flops, bytes_accessed=bytes_accessed, transcendentals=0)


def per_device(inputs, gates, cotangent, first_factor, second_factor):
    _, positions, channels = inputs.shape
    blocks, width_q, _ = first_factor.shape
    rows, width_p, _ = second_factor.shape
    owners = lax.axis_size("seq")
    shares = lax.axis_size("batch")
    packet = (owners, 2 * blocks * rows, channels)
    macs = positions * channels

    send = pl.pallas_call(
        send_kernel,
        grid=(channels // CHUNK,),
        in_specs=[sliced(inputs.shape)] * 3 + [whole(first_factor.shape), whole(second_factor.shape)],
        out_specs=sliced(packet),
        out_shape=jax.ShapeDtypeStruct(packet, BF16),
        scratch_shapes=[pltpu.VMEM((CHUNK // LANES, positions, LANES), F32)],
        compiler_params=pltpu.CompilerParams(vmem_limit_bytes=60 * MIB),
        cost_estimate=cost(2 * macs * (width_p + width_q), 6 * MIB),
        name="send",
    )(inputs, gates, cotangent, first_factor, second_factor)
    got = lax.all_to_all(send, "seq", 0, 0, tiled=True)

    lines = (blocks * width_q + rows * width_p // 2) // shares
    parts = pl.pallas_call(
        grads_kernel,
        in_specs=near(4),
        out_specs=pl.BlockSpec(memory_space=pltpu.VMEM),
        out_shape=jax.ShapeDtypeStruct((shares, lines, width_q), BF16),
        scratch_shapes=[pltpu.VMEM((channels // LANES, positions, LANES), F32)],
        compiler_params=pltpu.CompilerParams(vmem_limit_bytes=20 * MIB),
        cost_estimate=cost(2 * macs * (width_p + width_q), 6 * MIB),
        name="grads",
    )(got, inputs, gates, cotangent)
    sums = lax.all_to_all(parts, "batch", 0, 0, tiled=True)

    input_grad = pl.pallas_call(
        input_kernel,
        in_specs=near(2),
        out_specs=pl.BlockSpec(memory_space=pltpu.VMEM),
        out_shape=jax.ShapeDtypeStruct(inputs.shape, BF16),
        compiler_params=pltpu.CompilerParams(vmem_limit_bytes=20 * MIB),
        cost_estimate=cost(2 * macs * width_q, 3 * MIB),
        name="input",
    )(got, first_factor)

    first_grad, second_grad = pl.pallas_call(
        sum_kernel,
        in_specs=near(1),
        out_specs=near(2),
        out_shape=[
            jax.ShapeDtypeStruct((blocks, width_q // shares, width_q), F32),
            jax.ShapeDtypeStruct((rows, width_p // shares, width_p), F32),
        ],
        compiler_params=pltpu.CompilerParams(vmem_limit_bytes=20 * MIB),
        cost_estimate=cost(0, MIB),
        name="sums",
    )(sums)
    return input_grad, first_grad, second_grad


def solution(mesh):
    in_specs = (
        P("batch", "seq", None),
        P("batch", "seq", None),
        P("batch", "seq", None),
        P("seq", None, None),
        P("seq", None, None),
    )
    out_specs = (P("batch", "seq", None), P("seq", "batch", None), P("seq", "batch", None))
    return jax.shard_map(
        per_device, mesh=mesh, in_specs=in_specs, out_specs=out_specs, check_vma=False
    )
```

time: 246 us -> 103 us (0.42)
  the two profiles are of different devices: /device:TPU:6 before, /device:TPU:8 now
where the time goes in v1:
time: 103 us
  blocking collectives  63.4 us (62%)
  waiting for transfers between devices  20.2 us (20%)
  starting transfers between devices  10.4 us (10%)
  Pallas kernels  7.06 us (7%)
    all_to_all x1, blocking collectives, per_device(): got = lax.all_to_all(send, 'seq', 0, 0, tiled=True)  63.4 us
    all_to_all x1, waiting for transfers between devices, per_device(): sums = lax.all_to_all(parts, 'batch', 0, 0, tiled=True)  20.2 us
    all_to_all x1, starting transfers between devices, per_device(): sums = lax.all_to_all(parts, 'batch', 0, 0, tiled=True)  10.4 us
    pallas_call x1, Pallas kernels, per_device(): pl.pallas_call(send_kernel, grid=(channels // CHUNK,), in_specs=[sliced(i...  3.93 us
  transfers between devices with their start and end apart: 1, of which 1 were waited for; matrix products, arithmetic and copies ran while one was open for 0% of the time, Pallas kernels for 1%

profile of v1, /device:TPU:8, one launch (start us, length us, event | category | flops | bytes accessed | tf_op | source)
XLA Modules:
  0.0 102.7 jit_solution(13278788019274450860)
XLA Ops:
  0.6 3.9 %send.1 = bf16[32,64,512]{2,1,0:T(8,128)(2,1)} custom-call(bf16[1,1024,512]{2,1,0:T(8,128)(2,1)} %inputs.3, bf16[1,1024,512]{2,1,0:T(8,128)(2,1)} %gates.3, bf16[1,1024,512]{2,1,0:T(8,128)(2,1)} %cotangent.3, bf16[4,256,256]{2,1,0:T(8,128)(2,1)} %factor.1, bf16[8,128,128]{2,1,0:T(8,128)(2,1)} %second.1), custom_call_target="tpu_custom_call" | custom-call | flops 402653184 | bytes 6291456 | tf_op jit(solution)/shard_map/send/pallas_call | solution.py:124
  4.6 0.0 copy-start
  4.6 0.0 copy-start.1
  4.6 0.0 copy-start.2
  4.6 63.4 %all_to_all.10.got = bf16[32,64,512]{2,1,0:T(8,128)(2,1)S(1)} all-to-all(bf16[32,64,512]{2,1,0:T(8,128)(2,1)} %send.1), channel_id=1, replica_groups=mesh['seq'=32,'batch'=16] {'seq'}, dimensions={0} | all-to-all | bytes 4194304 | tf_op jit(solution)/shard_map/all_to_all | solution.py:135
  68.0 0.0 copy-done
  68.0 0.0 copy-done.1
  68.0 0.0 copy-done.2
  68.0 0.0 copy-start.4
  68.0 1.0 grads.1
  69.0 0.0 copy-start.3
  69.0 0.9 copy-done.3
  69.8 10.4 %all-to-all-start.1 = ((bf16[16,96,256]{2,1,0:T(8,128)(2,1)}), bf16[16,96,256]{2,1,0:T(8,128)(2,1)S(1)}, u32[]{:S(2)}, u32[]{:S(2)}) async-start(bf16[16,96,256]{2,1,0:T(8,128)(2,1)} %copy-done.3), calls=%async_computation.1 | async-start | bytes 1572864 | tf_op jit(solution)/shard_map/all_to_all | solution.py:148
  80.3 0.0 copy-done.4
  80.3 1.4 %input.1 = bf16[1,1024,512]{2,1,0:T(8,128)(2,1)} custom-call(bf16[32,64,512]{2,1,0:T(8,128)(2,1)S(1)} %all_to_all.10.got, bf16[4,256,256]{2,1,0:T(8,128)(2,1)S(1)} %copy-done.4), custom_call_target="tpu_custom_call" | custom-call | flops 268435456 | bytes 3145728 | tf_op jit(solution)/shard_map/input/pallas_call | solution.py:150
  81.7 20.2 %all-to-all-done.1.got = bf16[16,96,256]{2,1,0:T(8,128)(2,1)S(1)} async-done(((bf16[16,96,256]{2,1,0:T(8,128)(2,1)}), bf16[16,96,256]{2,1,0:T(8,128)(2,1)S(1)}, u32[]{:S(2)}, u32[]{:S(2)}) %all-to-all-start.1) | async-done | bytes 786464 | tf_op jit(solution)/shard_map/all_to_all | solution.py:148
  102.0 0.7 sums.1
Async XLA Ops:
  4.6 63.4 %copy-start = (bf16[1,1024,512]{2,1,0:T(8,128)(2,1)S(1)}, bf16[1,1024,512]{2,1,0:T(8,128)(2,1)}, u32[]{:S(2)}) copy-start(bf16[1,1024,512]{2,1,0:T(8,128)(2,1)} %inputs.3) | copy-start | bytes 3145732
  4.6 63.4 %copy-start.1 = (bf16[1,1024,512]{2,1,0:T(8,128)(2,1)S(1)}, bf16[1,1024,512]{2,1,0:T(8,128)(2,1)}, u32[]{:S(2)}) copy-start(bf16[1,1024,512]{2,1,0:T(8,128)(2,1)} %gates.3) | copy-start | bytes 3145732
  4.6 63.4 %copy-start.2 = (bf16[1,1024,512]{2,1,0:T(8,128)(2,1)S(1)}, bf16[1,1024,512]{2,1,0:T(8,128)(2,1)}, u32[]{:S(2)}) copy-start(bf16[1,1024,512]{2,1,0:T(8,128)(2,1)} %cotangent.3) | copy-start | bytes 3145732
  68.0 12.3 %copy-start.4 = (bf16[4,256,256]{2,1,0:T(8,128)(2,1)S(1)}, bf16[4,256,256]{2,1,0:T(8,128)(2,1)}, u32[]{:S(2)}) copy-start(bf16[4,256,256]{2,1,0:T(8,128)(2,1)} %factor.1) | copy-start | bytes 1572868
  69.0 0.9 copy-start.3
  69.8 32.1 %all-to-all-start.1 = ((bf16[16,96,256]{2,1,0:T(8,128)(2,1)}), bf16[16,96,256]{2,1,0:T(8,128)(2,1)S(1)}, u32[]{:S(2)}, u32[]{:S(2)}) async-start(bf16[16,96,256]{2,1,0:T(8,128)(2,1)} %copy-done.3), calls=%async_computation.1 | async-start | bytes 1572864 | tf_op jit(solution)/shard_map/all_to_all | solution.py:148

commit v2 on v0

v2 whole, which is shorter than its diff:
```python
import jax
import jax.numpy as jnp
from jax import lax
from jax.experimental import pallas as pl
from jax.experimental.pallas import tpu as pltpu
from jax.sharding import PartitionSpec as P

F32 = jnp.float32
BF16 = jnp.bfloat16
CHUNK = 256
LANES = 128
MIB = 1024 * 1024
LONG = 1 << 36


def dot(a, b, contract_a, contract_b):
    return lax.dot_general(a, b, (((contract_a,), (contract_b,)), ((), ())), preferred_element_type=F32)


def product(cotangent, gates):
    return (cotangent.astype(F32) * gates.astype(F32)).astype(BF16)


def send_kernel(inputs, gates, cotangent, first, second, send, spread):
    rows, width_p, _ = second.shape
    blocks, width_q, _ = first.shape
    owners, lines, _ = send.shape
    lines //= 2
    lanes = spread.shape[0] // 2
    for q in range(rows):
        part = pl.ds(q * width_p, width_p)
        back = dot(second[q], product(cotangent[0, part, :], gates[0, part, :]), 0, 0)
        for lane in range(lanes):
            spread[lane, pl.ds(q, width_p, stride=rows), :] = back[:, lane * LANES:(lane + 1) * LANES]
    for p in range(blocks):
        mixed = dot(first[p], inputs[0, p * width_q:(p + 1) * width_q, :], 1, 0)
        for lane in range(lanes):
            spread[lanes + lane, pl.ds(p, width_q, stride=blocks), :] = (
                mixed[:, lane * LANES:(lane + 1) * LANES]
            )
    for half in range(2):
        for lane in range(lanes):
            send[:, half * lines:(half + 1) * lines, lane * LANES:(lane + 1) * LANES] = (
                spread[half * lanes + lane].reshape(owners, lines, LANES).astype(BF16)
            )


def share_kernel(side, inputs, gates, cotangent, own, other, gates_in, cotangent_in, inputs_in, scaled, sems):
    half = own.shape[0] // 2
    here = pl.ds(pl.multiple_of(side[0] * half, half), half)
    there = pl.ds(pl.multiple_of((1 - side[0]) * half, half), half)
    top, bottom = pl.ds(0, half), pl.ds(half, half)
    entering = [
        pltpu.make_async_copy(inputs.at[0], inputs_in, sems.at[0]),
        pltpu.make_async_copy(gates.at[0], gates_in, sems.at[1]),
        pltpu.make_async_copy(cotangent.at[0], cotangent_in, sems.at[2]),
    ]
    leaving = [
        pltpu.make_async_copy(inputs_in.at[there], other.at[top], sems.at[3]),
        pltpu.make_async_copy(inputs_in.at[here], own.at[top], sems.at[4]),
        pltpu.make_async_copy(scaled.at[there], other.at[bottom], sems.at[5]),
        pltpu.make_async_copy(scaled.at[here], own.at[bottom], sems.at[6]),
    ]
    for copy in entering:
        copy.start()
    entering[0].wait()
    leaving[0].start()
    leaving[1].start()
    entering[1].wait()
    entering[2].wait()
    scaled[...] = product(cotangent_in[...], gates_in[...])
    leaving[2].start()
    leaving[3].start()
    for copy in leaving:
        copy.wait()


def theirs_kernel(side, after, got, theirs):
    owners, _, lines, channels = got.shape
    theirs[...] = got[:, pl.ds(1 - side[0], 1), :lines // 2, :].reshape(theirs.shape)


def grads_kernel(side, after, got, own, came, out, parts_in, spread, sems):
    owners, _, lines, channels = got.shape
    lines //= 2
    shares, height, width_q = out.shape
    width_p = LANES
    half = own.shape[0] // 2
    rows = half // width_p
    blocks = half // width_q
    depth = lines // rows
    lanes = channels // LANES
    cut = blocks * width_q // shares
    leaving = [
        pltpu.make_async_copy(parts_in.at[:, part], out.at[:, part], sems.at[n])
        for n, part in enumerate((pl.ds(0, cut), pl.ds(cut, height - cut)))
    ]
    firsts = [None] * blocks
    for away in range(2):
        packet = got[:, pl.ds(side[0] ^ away, 1), :, :].reshape(owners, 2 * lines, channels).astype(F32)
        wide = packet[:, :lines].reshape(owners, blocks, lines // blocks, channels)
        backs = [wide[:, p].reshape(width_q, channels).astype(BF16) for p in range(blocks)]
        for lane in range(lanes):
            spread[away, lane] = (
                packet[:, lines:, lane * LANES:(lane + 1) * LANES].reshape(owners * lines, LANES)
            )
        for p in range(blocks):
            source = (own, came)[away][p * width_q:(p + 1) * width_q, :]
            grad = dot(backs[p], source, 1, 1)
            firsts[p] = grad if firsts[p] is None else firsts[p] + grad
    parts_in[:, :cut, :] = jnp.concatenate(
        [grad.reshape(shares, width_q // shares, width_q) for grad in firsts], axis=1
    ).astype(BF16)
    leaving[0].start()
    seconds = []
    for q in range(rows):
        total = None
        for away in range(2):
            mixed = jnp.concatenate([
                jnp.concatenate([
                    spread[away, lane, pl.ds(q * depth + p, owners, stride=lines), :] for lane in range(lanes)
                ], axis=1)
                for p in range(depth)
            ], axis=0).astype(BF16)
            left = (own, came)[away][half + q * width_p:half + (q + 1) * width_p, :]
            grad = dot(left, mixed, 1, 1)
            total = grad if total is None else total + grad
        seconds.append(total.reshape(shares, width_p // shares, width_p))
    parts_in[:, cut:, :] = jnp.concatenate([
        jnp.concatenate([seconds[q], seconds[q + rows // 2]], axis=2) for q in range(rows // 2)
    ], axis=1).astype(BF16)
    leaving[1].start()
    leaving[0].wait()
    leaving[1].wait()


def own_kernel(side, got, factor, out, out_in, sems):
    owners, _, lines, channels = got.shape
    blocks, width, _ = factor.shape
    half = blocks // 2
    packet = got[:, pl.ds(side[0], 1), :lines // 2, :].reshape(owners, lines // 2, channels)
    half_input(packet, factor, side[0], out_in)
    there = pl.ds(pl.multiple_of(side[0] * half * width, half * width), half * width)
    copy = pltpu.make_async_copy(out_in, out.at[0, there], sems.at[0])
    copy.start()
    copy.wait()


def other_kernel(side, came, factor, grad, out, out_in, sems):
    blocks, width, _ = factor.shape
    half = blocks // 2
    half_input(came[...], factor, 1 - side[0], out_in)
    there = pl.ds(pl.multiple_of((1 - side[0]) * half * width, half * width), half * width)
    copy = pltpu.make_async_copy(out_in, out.at[0, there], sems.at[0])
    copy.start()
    copy.wait()


def half_input(packet, factor, at, out):
    owners, lines, channels = packet.shape
    blocks, width, _ = factor.shape
    half = blocks // 2
    wide = packet.astype(F32).reshape(owners, half, lines // half, channels)
    for p in range(half):
        back = wide[:, p].reshape(width, channels).astype(BF16)
        out[p * width:(p + 1) * width, :] = dot(factor[at * half + p], back, 0, 0).astype(BF16)


def sum_kernel(got, first, second):
    shares = got.shape[0]
    blocks, height, width_q = first.shape
    rows, depth, width_p = second.shape
    cut = blocks // 2 * height
    owners = width_p // blocks
    row = lax.broadcasted_iota(jnp.int32, (width_p, width_p), 0)
    column = lax.broadcasted_iota(jnp.int32, (width_p, width_p), 1)
    order = ((row % owners) * blocks + row // owners == column).astype(F32)
    for half in range(2):
        total = got[half].astype(F32)
        for share in range(2 + half, shares, 2):
            total = total + got[share].astype(F32)
        total = total * (1.0 / shares)
        at = half * blocks // 2
        first[at:at + blocks // 2] = total[:cut].reshape(blocks // 2, height, width_q)
        for side in range(2):
            lines = lax.dot_general(
                total[cut:, side * width_p:(side + 1) * width_p], order, (((1,), (0,)), ((), ())),
                precision=lax.Precision.HIGHEST, preferred_element_type=F32,
            )
            at = half * rows // 2 + side * rows // 4
            second[at:at + rows // 4] = lines.reshape(rows // 4, depth, width_p)


def whole(shape):
    return pl.BlockSpec(shape, lambda i: (0,) * len(shape))


def sliced(shape):
    return pl.BlockSpec(shape[:-1] + (CHUNK,), lambda i: (0,) * (len(shape) - 1) + (i,))


def cost(flops, bytes_accessed):
    return pl.CostEstimate(flops=flops, bytes_accessed=bytes_accessed, transcendentals=0)


def local(kernel, name, operands, out, scratch=(), sems=0, flops=0, size=3, aliases=None, close=0, scalars=0, far=0):
    space = pltpu.HBM if sems else pltpu.VMEM
    scalars = 1 if sems else scalars
    lead = [pl.BlockSpec(memory_space=pltpu.SMEM)] * scalars + [pl.BlockSpec(memory_space=pltpu.HBM)] * far
    return pl.pallas_call(
        kernel,
        in_specs=lead
        + [pl.BlockSpec(memory_space=pltpu.VMEM)] * close
        + [pl.BlockSpec(memory_space=space)] * (len(operands) - len(lead) - close),
        out_specs=[pl.BlockSpec(memory_space=space)] * len(out),
        input_output_aliases=aliases or {},
        out_shape=[jax.ShapeDtypeStruct(shape, dtype) for shape, dtype in out],
        scratch_shapes=[pltpu.VMEM(shape, dtype) for shape, dtype in scratch]
        + [pltpu.SemaphoreType.DMA((sems,))] * bool(sems),
        compiler_params=pltpu.CompilerParams(vmem_limit_bytes=24 * MIB),
        cost_estimate=cost(flops, size * MIB),
        name=name,
    )(*operands)


def per_device(inputs, gates, cotangent, first_factor, second_factor):
    _, positions, channels = inputs.shape
    blocks, width_q, _ = first_factor.shape
    rows, width_p, _ = second_factor.shape
    owners = lax.axis_size("seq")
    shares = lax.axis_size("batch")
    lines = blocks * rows
    half = positions // 2
    macs = positions * channels
    side = (lax.axis_index("batch").astype(jnp.int32) % 2).reshape(1)
    groups = [
        [owner * shares + pair * 2 + of for owner in range(owners) for of in range(2)]
        for pair in range(shares // 2)
    ]

    def swap(x):
        return lax.ppermute(x, "batch", [(i, i ^ 1) for i in range(shares)])

    packet = (owners * 2, lines, channels)
    send = pl.pallas_call(
        send_kernel,
        grid=(channels // CHUNK,),
        in_specs=[sliced(inputs.shape)] * 3 + [whole(first_factor.shape), whole(second_factor.shape)],
        out_specs=sliced(packet),
        out_shape=jax.ShapeDtypeStruct(packet, BF16),
        scratch_shapes=[pltpu.VMEM((2 * CHUNK // LANES, positions, LANES), F32)],
        compiler_params=pltpu.CompilerParams(vmem_limit_bytes=60 * MIB),
        cost_estimate=cost(2 * macs * (width_p + width_q), 6 * MIB),
        name="send",
    )(inputs, gates, cotangent, first_factor, second_factor)
    got = lax.all_to_all(send, ("seq", "batch"), 0, 0, tiled=True, axis_index_groups=groups)

    full = ((positions, channels), BF16)
    halved = ((half, channels), BF16)
    own, other = local(
        share_kernel, "share", (side, inputs, gates, cotangent), [full] * 2, [full] * 4, 7, 0, 5,
    )
    came = swap(other)

    height = (blocks * width_q + rows * width_p // 2) // 2 // shares
    got = got.reshape(owners, 2, lines, channels)
    [theirs] = local(
        theirs_kernel, "theirs", (side, came, got), [((owners, lines // 2, channels), BF16)], (), 0, 0, 1, None, 1, 1, 1,
    )
    [parts] = local(
        grads_kernel, "grads", (side, theirs, got, own, came),
        [((shares, height, width_q), BF16)],
        [((shares, height, width_q), BF16), ((2, channels // LANES, owners * lines // 2, LANES), F32)],
        2, 2 * macs * (width_p + width_q), 6, None, 3, 1, 1,
    )
    sums = lax.all_to_all(parts, "batch", 0, 0, tiled=True)
    [input_grad] = local(
        own_kernel, "own", (side, got, first_factor), [(inputs.shape, BF16)], [halved], 1, macs * width_q, 2,
        None, 2,
    )
    [input_grad] = local(
        other_kernel, "other", (side, swap(theirs), first_factor, input_grad), [(inputs.shape, BF16)], [halved],
        1, LONG, 2, {3: 0}, 2,
    )
    first_grad, second_grad = local(
        sum_kernel, "sums", (sums,),
        [
            ((blocks, width_q // shares, width_q), F32),
            ((rows, width_p // shares, width_p), F32),
        ], (), 0, 0, 1,
    )
    return input_grad, first_grad, second_grad


def solution(mesh):
    in_specs = (
        P("batch", "seq", None),
        P("batch", "seq", None),
        P("batch", "seq", None),
        P("seq", None, None),
        P("seq", None, None),
    )
    out_specs = (P("batch", "seq", None), P("seq", "batch", None), P("seq", "batch", None))
    return jax.shard_map(
        per_device, mesh=mesh, in_specs=in_specs, out_specs=out_specs, check_vma=False
    )
```

time: 246 us -> 99.4 us (0.40)
  the two profiles are of different devices: /device:TPU:6 before, /device:TPU:1 now
where the time goes in v2:
time: 99.4 us; the launch traced here: 98.9 us
  waiting for transfers between devices  51.6 us (52%)
  starting transfers between devices  30.4 us (31%)
  Pallas kernels  11.7 us (12%)
  local copies, waits for them, and re-layouts  4.45 us (4%)
    ppermute x2, waiting for transfers between devices, swap(): return lax.ppermute(x, 'batch', [(i, i ^ 1) for i in range(shares)])  41.3 us
    all_to_all x1, starting transfers between devices, per_device(): lax.all_to_all(send, ('seq', 'batch'), 0, 0, tiled=True, axis_index_group...  11.8 us
    all_to_all x1, starting transfers between devices, per_device(): sums = lax.all_to_all(parts, 'batch', 0, 0, tiled=True)  10.1 us
    all_to_all x1, waiting for transfers between devices, per_device(): sums = lax.all_to_all(parts, 'batch', 0, 0, tiled=True)  9.03 us
    ppermute x2, starting transfers between devices, swap(): return lax.ppermute(x, 'batch', [(i, i ^ 1) for i in range(shares)])  8.5 us
    pallas_call x6, Pallas kernels, local(): pl.pallas_call(kernel, in_specs=lead + [pl.BlockSpec(memory_space=pltpu.V...  7.66 us
    unnamed x12, local copies, waits for them, and re-layouts  4.45 us
    pallas_call x1, Pallas kernels, per_device(): pl.pallas_call(send_kernel, grid=(channels // CHUNK,), in_specs=[sliced(i...  4.03 us
  transfers between devices with their start and end apart: 4, of which 3 were waited for; matrix products, arithmetic and copies ran while one was open for 0% of the time, Pallas kernels for 6%

profile of v2, /device:TPU:1, one launch (start us, length us, event | category | flops | bytes accessed | tf_op | source)
XLA Modules:
  0.0 98.9 jit_solution(6731210199829987538)
XLA Ops:
  0.6 4.0 %send.1 = bf16[64,32,512]{2,1,0:T(8,128)(2,1)} custom-call(bf16[1,1024,512]{2,1,0:T(8,128)(2,1)} %inputs.3, bf16[1,1024,512]{2,1,0:T(8,128)(2,1)} %gates.3, bf16[1,1024,512]{2,1,0:T(8,128)(2,1)} %cotangent.3, bf16[4,256,256]{2,1,0:T(8,128)(2,1)} %factor.3, bf16[8,128,128]{2,1,0:T(8,128)(2,1)} %second.1), custom_call_target="tpu_custom_call" | custom-call | flops 402653184 | bytes 6291456 | tf_op jit(solution)/shard_map/send/pallas_call | solution.py:245
  4.7 0.0 copy-start
  4.7 11.8 %all-to-all-start = ((bf16[64,32,512]{2,1,0:T(8,128)(2,1)}), bf16[64,32,512]{2,1,0:T(8,128)(2,1)S(1)}, u32[]{:S(2)}, u32[]{:S(2)}) async-start(bf16[64,32,512]{2,1,0:T(8,128)(2,1)} %send.1), calls=%async_computation | async-start | bytes 4194304 | tf_op jit(solution)/shard_map/all_to_all | solution.py:256
  16.4 0.0 copy-done
  16.5 0.0 copy-start.1
  16.5 1.2 %copy-done.1 = bf16[1,1024,512]{2,1,0:T(8,128)(2,1)S(1)} copy-done((bf16[1,1024,512]{2,1,0:T(8,128)(2,1)S(1)}, bf16[1,1024,512]{2,1,0:T(8,128)(2,1)}, u32[]{:S(2)}) %copy-start.1) | copy-done | bytes 1048600
  17.7 0.0 copy-start.2
  17.7 1.2 %copy-done.2 = bf16[1,1024,512]{2,1,0:T(8,128)(2,1)S(1)} copy-done((bf16[1,1024,512]{2,1,0:T(8,128)(2,1)S(1)}, bf16[1,1024,512]{2,1,0:T(8,128)(2,1)}, u32[]{:S(2)}) %copy-start.2) | copy-done | bytes 1048600
  18.9 0.7 share.1
  19.6 0.0 copy-start.4
  19.6 1.0 copy-done.4
  20.6 3.3 %collective-permute-start = (bf16[1024,512]{1,0:T(8,128)(2,1)S(1)}, bf16[1024,512]{1,0:T(8,128)(2,1)S(1)}, u32[]{:S(2)}, u32[]{:S(2)}) collective-permute-start(bf16[1024,512]{1,0:T(8,128)(2,1)S(1)} %get-tuple-element.7), channel_id=1, source_target_pairs={{0,1},{1,0},{2,3},{3,2},{4,5},{5,4},{6,7},{7,6},{8,9},{9,8},{10,11... | collective-permute-start | bytes 3145736 | tf_op jit(solution)/shard_map/ppermute | solution.py:242
  23.8 41.3 %collective-permute-done.after.came = bf16[1024,512]{1,0:T(8,128)(2,1)S(1)} collective-permute-done((bf16[1024,512]{1,0:T(8,128)(2,1)S(1)}, bf16[1024,512]{1,0:T(8,128)(2,1)S(1)}, u32[]{:S(2)}, u32[]{:S(2)}) %collective-permute-start) | collective-permute-done | bytes 1048608 | tf_op jit(solution)/shard_map/ppermute | solution.py:242
  65.2 1.2 %all-to-all-done = bf16[64,32,512]{2,1,0:T(8,128)(2,1)S(1)} async-done(((bf16[64,32,512]{2,1,0:T(8,128)(2,1)}), bf16[64,32,512]{2,1,0:T(8,128)(2,1)S(1)}, u32[]{:S(2)}, u32[]{:S(2)}) %all-to-all-start) | async-done | bytes 2097184 | tf_op jit(solution)/shard_map/all_to_all | solution.py:256
  66.4 0.0 copy-start.5
  66.4 0.8 theirs.1.after
  67.2 5.2 %collective-permute-start.1 = (bf16[32,16,512]{2,1,0:T(8,128)(2,1)}, bf16[32,16,512]{2,1,0:T(8,128)(2,1)}, u32[]{:S(2)}, u32[]{:S(2)}) collective-permute-start(bf16[32,16,512]{2,1,0:T(8,128)(2,1)} %theirs.1.after), channel_id=1, source_target_pairs={{0,1},{1,0},{2,3},{3,2},{4,5},{5,4},{6,7},{7,6},{8,9},{9,8},{10,11... | collective-permute-start | bytes 1572872 | tf_op jit(solution)/shard_map/ppermute | solution.py:242
  72.5 0.0 copy-done.5
  72.5 1.9 %grads.1 = bf16[16,48,256]{2,1,0:T(8,128)(2,1)} custom-call(s32[1]{0:T(128)} %bitcast.side, bf16[32,16,512]{2,1,0:T(8,128)(2,1)} %theirs.1.after, bf16[32,2,32,512]{3,2,1,0:T(8,128)(2,1)S(1)} %bitcast.3, bf16[1024,512]{1,0:T(8,128)(2,1)S(1)} %copy-done.5, bf16[1024,512]{1,0:T(8,128)(2,1)S(1)} %collective-permute-done.after.came), custom_call_target="tpu_custom_call" | custom-call | flops 402653184 | bytes 6291456 | tf_op jit(solution)/shard_map/grads/pallas_call | solution.py:210
  74.4 10.1 %all-to-all-start.1 = ((bf16[16,48,256]{2,1,0:T(8,128)(2,1)}), bf16[16,48,256]{2,1,0:T(8,128)(2,1)S(1)}, u32[]{:S(2)}, u32[]{:S(2)}) async-start(bf16[16,48,256]{2,1,0:T(8,128)(2,1)} %grads.1), calls=%async_computation.1 | async-start | bytes 786432 | tf_op jit(solution)/shard_map/all_to_all | solution.py:276
  84.6 0.0 copy-start.3
  84.6 1.0 %copy-done.3 = bf16[4,256,256]{2,1,0:T(8,128)(2,1)S(1)} copy-done((bf16[4,256,256]{2,1,0:T(8,128)(2,1)S(1)}, bf16[4,256,256]{2,1,0:T(8,128)(2,1)}, u32[]{:S(2)}) %copy-start.3) | copy-done | bytes 524312
  85.6 1.1 %own.1.grad = bf16[1,1024,512]{2,1,0:T(8,128)(2,1)} custom-call(s32[1]{0:T(128)} %bitcast.side, bf16[32,2,32,512]{3,2,1,0:T(8,128)(2,1)S(1)} %bitcast.4, bf16[4,256,256]{2,1,0:T(8,128)(2,1)S(1)} %copy-done.3), custom_call_target="tpu_custom_call" | custom-call | flops 134217728 | bytes 2097152 | tf_op jit(solution)/shard_map/own/pallas_call | solution.py:210
  86.7 0.0 collective-permute-done.1.came
  86.7 2.2 %other.1 = bf16[1,1024,512]{2,1,0:T(8,128)(2,1)} custom-call(s32[1]{0:T(128)} %bitcast.side, bf16[32,16,512]{2,1,0:T(8,128)(2,1)} %collective-permute-done.1.came, bf16[4,256,256]{2,1,0:T(8,128)(2,1)S(1)} %copy-done.3, bf16[1,1024,512]{2,1,0:T(8,128)(2,1)} %own.1.grad), custom_call_target="tpu_custom_call", output_to_operand_aliasing={{}: (3, {})} | custom-call | flops 68719476736 | bytes 2097152 | tf_op jit(solution)/shard_map/other/pallas_call | solution.py:210
  88.9 9.0 %all-to-all-done.1.got = bf16[16,48,256]{2,1,0:T(8,128)(2,1)S(1)} async-done(((bf16[16,48,256]{2,1,0:T(8,128)(2,1)}), bf16[16,48,256]{2,1,0:T(8,128)(2,1)S(1)}, u32[]{:S(2)}, u32[]{:S(2)}) %all-to-all-start.1) | async-done | bytes 393248 | tf_op jit(solution)/shard_map/all_to_all | solution.py:276
  98.0 0.9 sums.1
Async XLA Ops:
  4.7 11.8 %copy-start = (bf16[1,1024,512]{2,1,0:T(8,128)(2,1)S(1)}, bf16[1,1024,512]{2,1,0:T(8,128)(2,1)}, u32[]{:S(2)}) copy-start(bf16[1,1024,512]{2,1,0:T(8,128)(2,1)} %inputs.3) | copy-start | bytes 3145732
  4.7 61.8 %all-to-all-start = ((bf16[64,32,512]{2,1,0:T(8,128)(2,1)}), bf16[64,32,512]{2,1,0:T(8,128)(2,1)S(1)}, u32[]{:S(2)}, u32[]{:S(2)}) async-start(bf16[64,32,512]{2,1,0:T(8,128)(2,1)} %send.1), calls=%async_computation | async-start | bytes 4194304 | tf_op jit(solution)/shard_map/all_to_all | solution.py:256
  16.5 1.2 %copy-start.1 = (bf16[1,1024,512]{2,1,0:T(8,128)(2,1)S(1)}, bf16[1,1024,512]{2,1,0:T(8,128)(2,1)}, u32[]{:S(2)}) copy-start(bf16[1,1024,512]{2,1,0:T(8,128)(2,1)} %gates.3) | copy-start | bytes 3145732
  17.7 1.2 %copy-start.2 = (bf16[1,1024,512]{2,1,0:T(8,128)(2,1)S(1)}, bf16[1,1024,512]{2,1,0:T(8,128)(2,1)}, u32[]{:S(2)}) copy-start(bf16[1,1024,512]{2,1,0:T(8,128)(2,1)} %cotangent.3) | copy-start | bytes 3145732
  19.6 1.0 copy-start.4
  20.6 44.6 %collective-permute-start = (bf16[1024,512]{1,0:T(8,128)(2,1)S(1)}, bf16[1024,512]{1,0:T(8,128)(2,1)S(1)}, u32[]{:S(2)}, u32[]{:S(2)}) collective-permute-start(bf16[1024,512]{1,0:T(8,128)(2,1)S(1)} %get-tuple-element.7), channel_id=1, source_target_pairs={{0,1},{1,0},{2,3},{3,2},{4,5},{5,4},{6,7},{7,6},{8,9},{9,8},{10,11... | collective-permute-start | bytes 3145736 | tf_op jit(solution)/shard_map/ppermute | solution.py:242
  66.4 6.1 %copy-start.5 = (bf16[1024,512]{1,0:T(8,128)(2,1)S(1)}, bf16[1024,512]{1,0:T(8,128)(2,1)}, u32[]{:S(2)}) copy-start(bf16[1024,512]{1,0:T(8,128)(2,1)} %copy-done.4) | copy-start | bytes 3145732
  67.2 19.5 %collective-permute-start.1 = (bf16[32,16,512]{2,1,0:T(8,128)(2,1)}, bf16[32,16,512]{2,1,0:T(8,128)(2,1)}, u32[]{:S(2)}, u32[]{:S(2)}) collective-permute-start(bf16[32,16,512]{2,1,0:T(8,128)(2,1)} %theirs.1.after), channel_id=1, source_target_pairs={{0,1},{1,0},{2,3},{3,2},{4,5},{5,4},{6,7},{7,6},{8,9},{9,8},{10,11... | collective-permute-start | bytes 1572872 | tf_op jit(solution)/shard_map/ppermute | solution.py:242
  74.4 23.5 %all-to-all-start.1 = ((bf16[16,48,256]{2,1,0:T(8,128)(2,1)}), bf16[16,48,256]{2,1,0:T(8,128)(2,1)S(1)}, u32[]{:S(2)}, u32[]{:S(2)}) async-start(bf16[16,48,256]{2,1,0:T(8,128)(2,1)} %grads.1), calls=%async_computation.1 | async-start | bytes 786432 | tf_op jit(solution)/shard_map/all_to_all | solution.py:276
  84.6 1.0 %copy-start.3 = (bf16[4,256,256]{2,1,0:T(8,128)(2,1)S(1)}, bf16[4,256,256]{2,1,0:T(8,128)(2,1)}, u32[]{:S(2)}) copy-start(bf16[4,256,256]{2,1,0:T(8,128)(2,1)} %factor.3) | copy-start | bytes 1572868

commit v3 on v2

--- a/solution.py
+++ b/solution.py
@@ -203,7 +203,7 @@
     return pl.CostEstimate(flops=flops, bytes_accessed=bytes_accessed, transcendentals=0)
 
 
-def local(kernel, name, operands, out, scratch=(), sems=0, flops=0, size=3, aliases=None, close=0, scalars=0, far=0):
+def local(kernel, name, operands, out, scratch=(), sems=0, flops=0, size=3, aliases=None, close=0, scalars=0, far=0, limit=24 * MIB):
     space = pltpu.HBM if sems else pltpu.VMEM
     scalars = 1 if sems else scalars
     lead = [pl.BlockSpec(memory_space=pltpu.SMEM)] * scalars + [pl.BlockSpec(memory_space=pltpu.HBM)] * far
@@ -217,7 +217,7 @@
         out_shape=[jax.ShapeDtypeStruct(shape, dtype) for shape, dtype in out],
         scratch_shapes=[pltpu.VMEM(shape, dtype) for shape, dtype in scratch]
         + [pltpu.SemaphoreType.DMA((sems,))] * bool(sems),
-        compiler_params=pltpu.CompilerParams(vmem_limit_bytes=24 * MIB),
+        compiler_params=pltpu.CompilerParams(vmem_limit_bytes=limit),
         cost_estimate=cost(flops, size * MIB),
         name=name,
     )(*operands)
@@ -258,7 +258,7 @@
     full = ((positions, channels), BF16)
     halved = ((half, channels), BF16)
     own, other = local(
-        share_kernel, "share", (side, inputs, gates, cotangent), [full] * 2, [full] * 4, 7, 0, 5,
+        share_kernel, "share", (side, inputs, gates, cotangent), [full] * 2, [full] * 4, 7, 0, 5, limit=60 * MIB,
     )
     came = swap(other)
 

time: 99.4 us -> 99.2 us (level)
  local copies, waits for them, and re-layouts: 4.45 us -> 1.04 us
  Pallas kernels: 11.7 us -> 14.1 us
  waiting for transfers between devices: 51.6 us -> 52.6 us
    unnamed x12 -> x4, local copies, waits for them, and re-layouts: 4.45 us -> 1.04 us
    pallas_call x6, Pallas kernels: 7.66 us -> 10.1 us  [local(): pl.pallas_call(kernel, in_specs=lead + [pl.BlockSpec(memory_space=pltpu.V...]
    all_to_all x1, waiting for transfers between devices: 1.24 us -> 2.36 us  [per_device(): lax.all_to_all(send, ('seq', 'batch'), 0, 0, tiled=True, axis_index_group...]
  transfers between devices with their start and end apart: 4 -> 4, of which waited for: 3 -> 3; matrix products, arithmetic and copies ran while one was open for 0% -> 0% of each run, Pallas kernels for 6% -> 8%
where the time goes in v3:
time: 99.2 us; the launch traced here: 98.8 us
  waiting for transfers between devices  52.6 us (53%)
  starting transfers between devices  30.3 us (31%)
  Pallas kernels  14.1 us (14%)
  local copies, waits for them, and re-layouts  1.04 us (1%)
    ppermute x2, waiting for transfers between devices, swap(): return lax.ppermute(x, 'batch', [(i, i ^ 1) for i in range(shares)])  41.2 us
    all_to_all x1, starting transfers between devices, per_device(): lax.all_to_all(send, ('seq', 'batch'), 0, 0, tiled=True, axis_index_group...  11.6 us
    all_to_all x1, starting transfers between devices, per_device(): sums = lax.all_to_all(parts, 'batch', 0, 0, tiled=True)  10.1 us
    pallas_call x6, Pallas kernels, local(): pl.pallas_call(kernel, in_specs=lead + [pl.BlockSpec(memory_space=pltpu.V...  10.1 us
    all_to_all x1, waiting for transfers between devices, per_device(): sums = lax.all_to_all(parts, 'batch', 0, 0, tiled=True)  9.04 us
    ppermute x2, starting transfers between devices, swap(): return lax.ppermute(x, 'batch', [(i, i ^ 1) for i in range(shares)])  8.52 us
    pallas_call x1, Pallas kernels, per_device(): pl.pallas_call(send_kernel, grid=(channels // CHUNK,), in_specs=[sliced(i...  4.02 us
    all_to_all x1, waiting for transfers between devices, per_device(): lax.all_to_all(send, ('seq', 'batch'), 0, 0, tiled=True, axis_index_group...  2.36 us
  transfers between devices with their start and end apart: 4, of which 3 were waited for; matrix products, arithmetic and copies ran while one was open for 0% of the time, Pallas kernels for 8%

profile of v3, /device:TPU:1, one launch (start us, length us, event | category | flops | bytes accessed | tf_op | source)
XLA Modules:
  0.0 98.8 jit_solution(18269175988156032516)
XLA Ops:
  0.6 4.0 %send.1 = bf16[64,32,512]{2,1,0:T(8,128)(2,1)} custom-call(bf16[1,1024,512]{2,1,0:T(8,128)(2,1)} %inputs.3, bf16[1,1024,512]{2,1,0:T(8,128)(2,1)} %gates.3, bf16[1,1024,512]{2,1,0:T(8,128)(2,1)} %cotangent.3, bf16[4,256,256]{2,1,0:T(8,128)(2,1)} %factor.3, bf16[8,128,128]{2,1,0:T(8,128)(2,1)} %second.1), custom_call_target="tpu_custom_call" | custom-call | flops 402653184 | bytes 6291456 | tf_op jit(solution)/shard_map/send/pallas_call | solution.py:245
  4.6 11.6 %all-to-all-start = ((bf16[64,32,512]{2,1,0:T(8,128)(2,1)}), bf16[64,32,512]{2,1,0:T(8,128)(2,1)S(1)}, u32[]{:S(2)}, u32[]{:S(2)}) async-start(bf16[64,32,512]{2,1,0:T(8,128)(2,1)} %send.1), calls=%async_computation | async-start | bytes 4194304 | tf_op jit(solution)/shard_map/all_to_all | solution.py:256
  16.3 3.1 %share.1 = (bf16[1024,512]{1,0:T(8,128)(2,1)}, bf16[1024,512]{1,0:T(8,128)(2,1)}) custom-call(s32[1]{0:T(128)} %bitcast.side, bf16[1,1024,512]{2,1,0:T(8,128)(2,1)} %inputs.3, bf16[1,1024,512]{2,1,0:T(8,128)(2,1)} %gates.3, bf16[1,1024,512]{2,1,0:T(8,128)(2,1)} %cotangent.3), custom_call_target="tpu_custom_call" | custom-call | bytes 5242880 | tf_op jit(solution)/shard_map/share/pallas_call | solution.py:210
  19.4 3.3 %collective-permute-start = (bf16[1024,512]{1,0:T(8,128)(2,1)}, bf16[1024,512]{1,0:T(8,128)(2,1)S(1)}, u32[]{:S(2)}, u32[]{:S(2)}) collective-permute-start(bf16[1024,512]{1,0:T(8,128)(2,1)} %get-tuple-element.7), channel_id=1, source_target_pairs={{0,1},{1,0},{2,3},{3,2},{4,5},{5,4},{6,7},{7,6},{8,9},{9,8},{10,11... | collective-permute-start | bytes 3145736 | tf_op jit(solution)/shard_map/ppermute | solution.py:242
  22.7 41.2 %collective-permute-done.after.came = bf16[1024,512]{1,0:T(8,128)(2,1)S(1)} collective-permute-done((bf16[1024,512]{1,0:T(8,128)(2,1)}, bf16[1024,512]{1,0:T(8,128)(2,1)S(1)}, u32[]{:S(2)}, u32[]{:S(2)}) %collective-permute-start) | collective-permute-done | bytes 1048608 | tf_op jit(solution)/shard_map/ppermute | solution.py:242
  63.9 2.4 %all-to-all-done = bf16[64,32,512]{2,1,0:T(8,128)(2,1)S(1)} async-done(((bf16[64,32,512]{2,1,0:T(8,128)(2,1)}), bf16[64,32,512]{2,1,0:T(8,128)(2,1)S(1)}, u32[]{:S(2)}, u32[]{:S(2)}) %all-to-all-start) | async-done | bytes 2097184 | tf_op jit(solution)/shard_map/all_to_all | solution.py:256
  66.3 0.0 copy-start.1
  66.3 0.8 theirs.1.after
  67.1 5.2 %collective-permute-start.1 = (bf16[32,16,512]{2,1,0:T(8,128)(2,1)}, bf16[32,16,512]{2,1,0:T(8,128)(2,1)}, u32[]{:S(2)}, u32[]{:S(2)}) collective-permute-start(bf16[32,16,512]{2,1,0:T(8,128)(2,1)} %theirs.1.after), channel_id=1, source_target_pairs={{0,1},{1,0},{2,3},{3,2},{4,5},{5,4},{6,7},{7,6},{8,9},{9,8},{10,11... | collective-permute-start | bytes 1572872 | tf_op jit(solution)/shard_map/ppermute | solution.py:242
  72.3 0.0 copy-done.1
  72.3 1.9 %grads.1 = bf16[16,48,256]{2,1,0:T(8,128)(2,1)} custom-call(s32[1]{0:T(128)} %bitcast.side, bf16[32,16,512]{2,1,0:T(8,128)(2,1)} %theirs.1.after, bf16[32,2,32,512]{3,2,1,0:T(8,128)(2,1)S(1)} %bitcast.3, bf16[1024,512]{1,0:T(8,128)(2,1)S(1)} %copy-done.1, bf16[1024,512]{1,0:T(8,128)(2,1)S(1)} %collective-permute-done.after.came), custom_call_target="tpu_custom_call" | custom-call | flops 402653184 | bytes 6291456 | tf_op jit(solution)/shard_map/grads/pallas_call | solution.py:210
  74.3 10.1 %all-to-all-start.1 = ((bf16[16,48,256]{2,1,0:T(8,128)(2,1)}), bf16[16,48,256]{2,1,0:T(8,128)(2,1)S(1)}, u32[]{:S(2)}, u32[]{:S(2)}) async-start(bf16[16,48,256]{2,1,0:T(8,128)(2,1)} %grads.1), calls=%async_computation.1 | async-start | bytes 786432 | tf_op jit(solution)/shard_map/all_to_all | solution.py:276
  84.4 0.0 copy-start
  84.4 1.0 %copy-done = bf16[4,256,256]{2,1,0:T(8,128)(2,1)S(1)} copy-done((bf16[4,256,256]{2,1,0:T(8,128)(2,1)S(1)}, bf16[4,256,256]{2,1,0:T(8,128)(2,1)}, u32[]{:S(2)}) %copy-start) | copy-done | bytes 524312
  85.5 1.1 %own.1.grad = bf16[1,1024,512]{2,1,0:T(8,128)(2,1)} custom-call(s32[1]{0:T(128)} %bitcast.side, bf16[32,2,32,512]{3,2,1,0:T(8,128)(2,1)S(1)} %bitcast.4, bf16[4,256,256]{2,1,0:T(8,128)(2,1)S(1)} %copy-done), custom_call_target="tpu_custom_call" | custom-call | flops 134217728 | bytes 2097152 | tf_op jit(solution)/shard_map/own/pallas_call | solution.py:210
  86.6 0.0 collective-permute-done.1.came
  86.6 2.2 %other.1 = bf16[1,1024,512]{2,1,0:T(8,128)(2,1)} custom-call(s32[1]{0:T(128)} %bitcast.side, bf16[32,16,512]{2,1,0:T(8,128)(2,1)} %collective-permute-done.1.came, bf16[4,256,256]{2,1,0:T(8,128)(2,1)S(1)} %copy-done, bf16[1,1024,512]{2,1,0:T(8,128)(2,1)} %own.1.grad), custom_call_target="tpu_custom_call", output_to_operand_aliasing={{}: (3, {})} | custom-call | flops 68719476736 | bytes 2097152 | tf_op jit(solution)/shard_map/other/pallas_call | solution.py:210
  88.8 9.0 %all-to-all-done.1.got = bf16[16,48,256]{2,1,0:T(8,128)(2,1)S(1)} async-done(((bf16[16,48,256]{2,1,0:T(8,128)(2,1)}), bf16[16,48,256]{2,1,0:T(8,128)(2,1)S(1)}, u32[]{:S(2)}, u32[]{:S(2)}) %all-to-all-start.1) | async-done | bytes 393248 | tf_op jit(solution)/shard_map/all_to_all | solution.py:276
  97.8 0.9 sums.1
Async XLA Ops:
  4.6 61.6 %all-to-all-start = ((bf16[64,32,512]{2,1,0:T(8,128)(2,1)}), bf16[64,32,512]{2,1,0:T(8,128)(2,1)S(1)}, u32[]{:S(2)}, u32[]{:S(2)}) async-start(bf16[64,32,512]{2,1,0:T(8,128)(2,1)} %send.1), calls=%async_computation | async-start | bytes 4194304 | tf_op jit(solution)/shard_map/all_to_all | solution.py:256
  19.4 44.5 %collective-permute-start = (bf16[1024,512]{1,0:T(8,128)(2,1)}, bf16[1024,512]{1,0:T(8,128)(2,1)S(1)}, u32[]{:S(2)}, u32[]{:S(2)}) collective-permute-start(bf16[1024,512]{1,0:T(8,128)(2,1)} %get-tuple-element.7), channel_id=1, source_target_pairs={{0,1},{1,0},{2,3},{3,2},{4,5},{5,4},{6,7},{7,6},{8,9},{9,8},{10,11... | collective-permute-start | bytes 3145736 | tf_op jit(solution)/shard_map/ppermute | solution.py:242
  66.3 6.1 %copy-start.1 = (bf16[1024,512]{1,0:T(8,128)(2,1)S(1)}, bf16[1024,512]{1,0:T(8,128)(2,1)}, u32[]{:S(2)}) copy-start(bf16[1024,512]{1,0:T(8,128)(2,1)} %get-tuple-element.8.own) | copy-start | bytes 3145732
  67.1 19.5 %collective-permute-start.1 = (bf16[32,16,512]{2,1,0:T(8,128)(2,1)}, bf16[32,16,512]{2,1,0:T(8,128)(2,1)}, u32[]{:S(2)}, u32[]{:S(2)}) collective-permute-start(bf16[32,16,512]{2,1,0:T(8,128)(2,1)} %theirs.1.after), channel_id=1, source_target_pairs={{0,1},{1,0},{2,3},{3,2},{4,5},{5,4},{6,7},{7,6},{8,9},{9,8},{10,11... | collective-permute-start | bytes 1572872 | tf_op jit(solution)/shard_map/ppermute | solution.py:242
  74.3 23.5 %all-to-all-start.1 = ((bf16[16,48,256]{2,1,0:T(8,128)(2,1)}), bf16[16,48,256]{2,1,0:T(8,128)(2,1)S(1)}, u32[]{:S(2)}, u32[]{:S(2)}) async-start(bf16[16,48,256]{2,1,0:T(8,128)(2,1)} %grads.1), calls=%async_computation.1 | async-start | bytes 786432 | tf_op jit(solution)/shard_map/all_to_all | solution.py:276
  84.4 1.0 %copy-start = (bf16[4,256,256]{2,1,0:T(8,128)(2,1)S(1)}, bf16[4,256,256]{2,1,0:T(8,128)(2,1)}, u32[]{:S(2)}) copy-start(bf16[4,256,256]{2,1,0:T(8,128)(2,1)} %factor.3) | copy-start | bytes 1572868

commit v4 on v3

--- a/solution.py
+++ b/solution.py
@@ -80,7 +80,7 @@
     theirs[...] = got[:, pl.ds(1 - side[0], 1), :lines // 2, :].reshape(theirs.shape)
 
 
-def grads_kernel(side, after, got, own, came, out, parts_in, spread, sems):
+def grads_kernel(side, after, got, own, came, out, mine, parts_in, spread, sems):
     owners, _, lines, channels = got.shape
     lines //= 2
     shares, height, width_q = out.shape
@@ -95,6 +95,8 @@
         pltpu.make_async_copy(parts_in.at[:, part], out.at[:, part], sems.at[n])
         for n, part in enumerate((pl.ds(0, cut), pl.ds(cut, height - cut)))
     ]
+    leaving.append(pltpu.make_async_copy(got.at[:, side[0], pl.ds(0, lines)], mine, sems.at[2]))
+    leaving[2].start()
     firsts = [None] * blocks
     for away in range(2):
         packet = got[:, pl.ds(side[0] ^ away, 1), :, :].reshape(owners, 2 * lines, channels).astype(F32)
@@ -130,16 +132,14 @@
         jnp.concatenate([seconds[q], seconds[q + rows // 2]], axis=2) for q in range(rows // 2)
     ], axis=1).astype(BF16)
     leaving[1].start()
-    leaving[0].wait()
-    leaving[1].wait()
-
-
-def own_kernel(side, got, factor, out, out_in, sems):
-    owners, _, lines, channels = got.shape
+    for copy in leaving:
+        copy.wait()
+
+
+def own_kernel(side, kept, factor, out, out_in, sems):
     blocks, width, _ = factor.shape
     half = blocks // 2
-    packet = got[:, pl.ds(side[0], 1), :lines // 2, :].reshape(owners, lines // 2, channels)
-    half_input(packet, factor, side[0], out_in)
+    half_input(kept[...], factor, side[0], out_in)
     there = pl.ds(pl.multiple_of(side[0] * half * width, half * width), half * width)
     copy = pltpu.make_async_copy(out_in, out.at[0, there], sems.at[0])
     copy.start()
@@ -267,15 +267,15 @@
     [theirs] = local(
         theirs_kernel, "theirs", (side, came, got), [((owners, lines // 2, channels), BF16)], (), 0, 0, 1, None, 1, 1, 1,
     )
-    [parts] = local(
+    parts, kept = local(
         grads_kernel, "grads", (side, theirs, got, own, came),
-        [((shares, height, width_q), BF16)],
+        [((shares, height, width_q), BF16), ((owners, lines // 2, channels), BF16)],
         [((shares, height, width_q), BF16), ((2, channels // LANES, owners * lines // 2, LANES), F32)],
-        2, 2 * macs * (width_p + width_q), 6, None, 3, 1, 1,
+        3, 2 * macs * (width_p + width_q), 6, None, 3, 1, 1,
     )
     sums = lax.all_to_all(parts, "batch", 0, 0, tiled=True)
     [input_grad] = local(
-        own_kernel, "own", (side, got, first_factor), [(inputs.shape, BF16)], [halved], 1, macs * width_q, 2,
+        own_kernel, "own", (side, kept, first_factor), [(inputs.shape, BF16)], [halved], 1, macs * width_q, 2,
         None, 2,
     )
     [input_grad] = local(

time: 99.2 us -> 100 us (level)
  local copies, waits for them, and re-layouts: 1.04 us -> 2.87 us
  waiting for transfers between devices: 52.6 us -> 51.5 us
    unnamed x4 -> x8, local copies, waits for them, and re-layouts: 1.04 us -> 2.87 us
    all_to_all x1, waiting for transfers between devices: 9.04 us -> 7.99 us  [per_device(): sums = lax.all_to_all(parts, 'batch', 0, 0, tiled=True)]
where the time goes in v4:
time: 100 us; the launch traced here: 99.6 us
  waiting for transfers between devices  51.5 us (52%)
  starting transfers between devices  30.3 us (30%)
  Pallas kernels  14.2 us (14%)
  local copies, waits for them, and re-layouts  2.87 us (3%)
    ppermute x2, waiting for transfers between devices, swap(): return lax.ppermute(x, 'batch', [(i, i ^ 1) for i in range(shares)])  41.2 us
    all_to_all x1, starting transfers between devices, per_device(): lax.all_to_all(send, ('seq', 'batch'), 0, 0, tiled=True, axis_index_group...  11.6 us
    pallas_call x6, Pallas kernels, local(): pl.pallas_call(kernel, in_specs=lead + [pl.BlockSpec(memory_space=pltpu.V...  10.2 us
    all_to_all x1, starting transfers between devices, per_device(): sums = lax.all_to_all(parts, 'batch', 0, 0, tiled=True)  10.1 us
    ppermute x2, starting transfers between devices, swap(): return lax.ppermute(x, 'batch', [(i, i ^ 1) for i in range(shares)])  8.52 us
    all_to_all x1, waiting for transfers between devices, per_device(): sums = lax.all_to_all(parts, 'batch', 0, 0, tiled=True)  7.99 us
    pallas_call x1, Pallas kernels, per_device(): pl.pallas_call(send_kernel, grid=(channels // CHUNK,), in_specs=[sliced(i...  4.03 us
    unnamed x8, local copies, waits for them, and re-layouts  2.87 us
  transfers between devices with their start and end apart: 4, of which 3 were waited for; matrix products, arithmetic and copies ran while one was open for 0% of the time, Pallas kernels for 8%

profile of v4, /device:TPU:1, one launch (start us, length us, event | category | flops | bytes accessed | tf_op | source)
XLA Modules:
  0.0 99.6 jit_solution(118951773494481455)
XLA Ops:
  0.6 4.0 %send.1 = bf16[64,32,512]{2,1,0:T(8,128)(2,1)} custom-call(bf16[1,1024,512]{2,1,0:T(8,128)(2,1)} %inputs.3, bf16[1,1024,512]{2,1,0:T(8,128)(2,1)} %gates.3, bf16[1,1024,512]{2,1,0:T(8,128)(2,1)} %cotangent.3, bf16[4,256,256]{2,1,0:T(8,128)(2,1)} %factor.3, bf16[8,128,128]{2,1,0:T(8,128)(2,1)} %second.1), custom_call_target="tpu_custom_call" | custom-call | flops 402653184 | bytes 6291456 | tf_op jit(solution)/shard_map/send/pallas_call | solution.py:245
  4.7 11.6 %all-to-all-start = ((bf16[64,32,512]{2,1,0:T(8,128)(2,1)}), bf16[64,32,512]{2,1,0:T(8,128)(2,1)S(1)}, u32[]{:S(2)}, u32[]{:S(2)}) async-start(bf16[64,32,512]{2,1,0:T(8,128)(2,1)} %send.1), calls=%async_computation | async-start | bytes 4194304 | tf_op jit(solution)/shard_map/all_to_all | solution.py:256
  16.3 3.1 %share.1 = (bf16[1024,512]{1,0:T(8,128)(2,1)}, bf16[1024,512]{1,0:T(8,128)(2,1)}) custom-call(s32[1]{0:T(128)} %bitcast.side, bf16[1,1024,512]{2,1,0:T(8,128)(2,1)} %inputs.3, bf16[1,1024,512]{2,1,0:T(8,128)(2,1)} %gates.3, bf16[1,1024,512]{2,1,0:T(8,128)(2,1)} %cotangent.3), custom_call_target="tpu_custom_call" | custom-call | bytes 5242880 | tf_op jit(solution)/shard_map/share/pallas_call | solution.py:210
  19.4 3.3 %collective-permute-start = (bf16[1024,512]{1,0:T(8,128)(2,1)}, bf16[1024,512]{1,0:T(8,128)(2,1)S(1)}, u32[]{:S(2)}, u32[]{:S(2)}) collective-permute-start(bf16[1024,512]{1,0:T(8,128)(2,1)} %get-tuple-element.9), channel_id=1, source_target_pairs={{0,1},{1,0},{2,3},{3,2},{4,5},{5,4},{6,7},{7,6},{8,9},{9,8},{10,11... | collective-permute-start | bytes 3145736 | tf_op jit(solution)/shard_map/ppermute | solution.py:242
  22.7 41.2 %collective-permute-done.after.came = bf16[1024,512]{1,0:T(8,128)(2,1)S(1)} collective-permute-done((bf16[1024,512]{1,0:T(8,128)(2,1)}, bf16[1024,512]{1,0:T(8,128)(2,1)S(1)}, u32[]{:S(2)}, u32[]{:S(2)}) %collective-permute-start) | collective-permute-done | bytes 1048608 | tf_op jit(solution)/shard_map/ppermute | solution.py:242
  63.9 2.4 %all-to-all-done = bf16[64,32,512]{2,1,0:T(8,128)(2,1)S(1)} async-done(((bf16[64,32,512]{2,1,0:T(8,128)(2,1)}), bf16[64,32,512]{2,1,0:T(8,128)(2,1)S(1)}, u32[]{:S(2)}, u32[]{:S(2)}) %all-to-all-start) | async-done | bytes 2097184 | tf_op jit(solution)/shard_map/all_to_all | solution.py:256
  66.3 0.0 copy-start.1
  66.3 0.8 theirs.1.after
  67.1 5.2 %collective-permute-start.1 = (bf16[32,16,512]{2,1,0:T(8,128)(2,1)}, bf16[32,16,512]{2,1,0:T(8,128)(2,1)}, u32[]{:S(2)}, u32[]{:S(2)}) collective-permute-start(bf16[32,16,512]{2,1,0:T(8,128)(2,1)} %theirs.1.after), channel_id=1, source_target_pairs={{0,1},{1,0},{2,3},{3,2},{4,5},{5,4},{6,7},{7,6},{8,9},{9,8},{10,11... | collective-permute-start | bytes 1572872 | tf_op jit(solution)/shard_map/ppermute | solution.py:242
  72.4 0.0 copy-done.1
  72.4 2.0 %grads.1 = (bf16[16,48,256]{2,1,0:T(8,128)(2,1)}, bf16[32,16,512]{2,1,0:T(8,128)(2,1)S(1)}) custom-call(s32[1]{0:T(128)} %bitcast.side, bf16[32,16,512]{2,1,0:T(8,128)(2,1)} %theirs.1.after, bf16[32,2,32,512]{3,2,1,0:T(8,128)(2,1)S(1)} %bitcast.3, bf16[1024,512]{1,0:T(8,128)(2,1)S(1)} %copy-done.1, bf16[1024,512]{1,0:T(8,128)(2,1)S(1)} %collective-permute-done.after.came), custom_call_target="tpu_custom_call" | custom-call | flops 402653184 | bytes 6291456 | tf_op jit(solution)/shard_map/grads/pallas_call | solution.py:210
  74.4 0.0 copy-start.2
  74.4 0.8 copy-done.2
  75.2 10.1 %all-to-all-start.1 = ((bf16[16,48,256]{2,1,0:T(8,128)(2,1)}), bf16[16,48,256]{2,1,0:T(8,128)(2,1)S(1)}, u32[]{:S(2)}, u32[]{:S(2)}) async-start(bf16[16,48,256]{2,1,0:T(8,128)(2,1)} %get-tuple-element.12), calls=%async_computation.1 | async-start | bytes 786432 | tf_op jit(solution)/shard_map/all_to_all | solution.py:276
  85.3 0.0 copy-start
  85.3 1.0 %copy-done = bf16[4,256,256]{2,1,0:T(8,128)(2,1)S(1)} copy-done((bf16[4,256,256]{2,1,0:T(8,128)(2,1)S(1)}, bf16[4,256,256]{2,1,0:T(8,128)(2,1)}, u32[]{:S(2)}) %copy-start) | copy-done | bytes 524312
  86.3 0.0 copy-start.3
  86.3 1.0 %copy-done.3 = bf16[32,16,512]{2,1,0:T(8,128)(2,1)S(1)} copy-done((bf16[32,16,512]{2,1,0:T(8,128)(2,1)S(1)}, bf16[32,16,512]{2,1,0:T(8,128)(2,1)}, u32[]{:S(2)}) %copy-start.3) | copy-done | bytes 524312
  87.4 1.1 %own.1.grad = bf16[1,1024,512]{2,1,0:T(8,128)(2,1)} custom-call(s32[1]{0:T(128)} %bitcast.side, bf16[32,16,512]{2,1,0:T(8,128)(2,1)S(1)} %copy-done.3, bf16[4,256,256]{2,1,0:T(8,128)(2,1)S(1)} %copy-done), custom_call_target="tpu_custom_call" | custom-call | flops 134217728 | bytes 2097152 | tf_op jit(solution)/shard_map/own/pallas_call | solution.py:210
  88.5 0.0 collective-permute-done.1.came
  88.5 2.2 %other.1 = bf16[1,1024,512]{2,1,0:T(8,128)(2,1)} custom-call(s32[1]{0:T(128)} %bitcast.side, bf16[32,16,512]{2,1,0:T(8,128)(2,1)} %collective-permute-done.1.came, bf16[4,256,256]{2,1,0:T(8,128)(2,1)S(1)} %copy-done, bf16[1,1024,512]{2,1,0:T(8,128)(2,1)} %own.1.grad), custom_call_target="tpu_custom_call", output_to_operand_aliasing={{}: (3, {})} | custom-call | flops 68719476736 | bytes 2097152 | tf_op jit(solution)/shard_map/other/pallas_call | solution.py:210
  90.7 8.0 %all-to-all-done.1.got = bf16[16,48,256]{2,1,0:T(8,128)(2,1)S(1)} async-done(((bf16[16,48,256]{2,1,0:T(8,128)(2,1)}), bf16[16,48,256]{2,1,0:T(8,128)(2,1)S(1)}, u32[]{:S(2)}, u32[]{:S(2)}) %all-to-all-start.1) | async-done | bytes 393248 | tf_op jit(solution)/shard_map/all_to_all | solution.py:276
  98.7 0.9 sums.1
Async XLA Ops:
  4.7 61.6 %all-to-all-start = ((bf16[64,32,512]{2,1,0:T(8,128)(2,1)}), bf16[64,32,512]{2,1,0:T(8,128)(2,1)S(1)}, u32[]{:S(2)}, u32[]{:S(2)}) async-start(bf16[64,32,512]{2,1,0:T(8,128)(2,1)} %send.1), calls=%async_computation | async-start | bytes 4194304 | tf_op jit(solution)/shard_map/all_to_all | solution.py:256
  19.4 44.5 %collective-permute-start = (bf16[1024,512]{1,0:T(8,128)(2,1)}, bf16[1024,512]{1,0:T(8,128)(2,1)S(1)}, u32[]{:S(2)}, u32[]{:S(2)}) collective-permute-start(bf16[1024,512]{1,0:T(8,128)(2,1)} %get-tuple-element.9), channel_id=1, source_target_pairs={{0,1},{1,0},{2,3},{3,2},{4,5},{5,4},{6,7},{7,6},{8,9},{9,8},{10,11... | collective-permute-start | bytes 3145736 | tf_op jit(solution)/shard_map/ppermute | solution.py:242
  66.3 6.1 %copy-start.1 = (bf16[1024,512]{1,0:T(8,128)(2,1)S(1)}, bf16[1024,512]{1,0:T(8,128)(2,1)}, u32[]{:S(2)}) copy-start(bf16[1024,512]{1,0:T(8,128)(2,1)} %get-tuple-element.10.own) | copy-start | bytes 3145732
  67.1 21.4 %collective-permute-start.1 = (bf16[32,16,512]{2,1,0:T(8,128)(2,1)}, bf16[32,16,512]{2,1,0:T(8,128)(2,1)}, u32[]{:S(2)}, u32[]{:S(2)}) collective-permute-start(bf16[32,16,512]{2,1,0:T(8,128)(2,1)} %theirs.1.after), channel_id=1, source_target_pairs={{0,1},{1,0},{2,3},{3,2},{4,5},{5,4},{6,7},{7,6},{8,9},{9,8},{10,11... | collective-permute-start | bytes 1572872 | tf_op jit(solution)/shard_map/ppermute | solution.py:242
  74.4 0.8 copy-start.2
  75.2 23.5 %all-to-all-start.1 = ((bf16[16,48,256]{2,1,0:T(8,128)(2,1)}), bf16[16,48,256]{2,1,0:T(8,128)(2,1)S(1)}, u32[]{:S(2)}, u32[]{:S(2)}) async-start(bf16[16,48,256]{2,1,0:T(8,128)(2,1)} %get-tuple-element.12), calls=%async_computation.1 | async-start | bytes 786432 | tf_op jit(solution)/shard_map/all_to_all | solution.py:276
  85.3 1.0 %copy-start = (bf16[4,256,256]{2,1,0:T(8,128)(2,1)S(1)}, bf16[4,256,256]{2,1,0:T(8,128)(2,1)}, u32[]{:S(2)}) copy-start(bf16[4,256,256]{2,1,0:T(8,128)(2,1)} %factor.3) | copy-start | bytes 1572868
  86.3 1.0 %copy-start.3 = (bf16[32,16,512]{2,1,0:T(8,128)(2,1)S(1)}, bf16[32,16,512]{2,1,0:T(8,128)(2,1)}, u32[]{:S(2)}) copy-start(bf16[32,16,512]{2,1,0:T(8,128)(2,1)} %copy-done.2) | copy-start | bytes 1572868

commit v5 on v3

--- a/solution.py
+++ b/solution.py
@@ -175,6 +175,7 @@
     row = lax.broadcasted_iota(jnp.int32, (width_p, width_p), 0)
     column = lax.broadcasted_iota(jnp.int32, (width_p, width_p), 1)
     order = ((row % owners) * blocks + row // owners == column).astype(F32)
+    lines = []
     for half in range(2):
         total = got[half].astype(F32)
         for share in range(2 + half, shares, 2):
@@ -182,13 +183,11 @@
         total = total * (1.0 / shares)
         at = half * blocks // 2
         first[at:at + blocks // 2] = total[:cut].reshape(blocks // 2, height, width_q)
-        for side in range(2):
-            lines = lax.dot_general(
-                total[cut:, side * width_p:(side + 1) * width_p], order, (((1,), (0,)), ((), ())),
-                precision=lax.Precision.HIGHEST, preferred_element_type=F32,
-            )
-            at = half * rows // 2 + side * rows // 4
-            second[at:at + rows // 4] = lines.reshape(rows // 4, depth, width_p)
+        lines += [total[cut:, :width_p], total[cut:, width_p:]]
+    second[...] = lax.dot_general(
+        jnp.concatenate(lines, axis=0), order, (((1,), (0,)), ((), ())),
+        precision=lax.Precision.HIGHEST, preferred_element_type=F32,
+    ).reshape(second.shape)
 
 
 def whole(shape):

time: 99.2 us -> 99.1 us (level)
  no operation moved by 1% of the time
where the time goes in v5:
time: 99.1 us; the launch traced here: 98.6 us
  waiting for transfers between devices  52.6 us (53%)
  starting transfers between devices  30.3 us (31%)
  Pallas kernels  14 us (14%)
  local copies, waits for them, and re-layouts  1.04 us (1%)
    ppermute x2, waiting for transfers between devices, swap(): return lax.ppermute(x, 'batch', [(i, i ^ 1) for i in range(shares)])  41.2 us
    all_to_all x1, starting transfers between devices, per_device(): lax.all_to_all(send, ('seq', 'batch'), 0, 0, tiled=True, axis_index_group...  11.6 us
    all_to_all x1, starting transfers between devices, per_device(): sums = lax.all_to_all(parts, 'batch', 0, 0, tiled=True)  10.1 us
    pallas_call x6, Pallas kernels, local(): pl.pallas_call(kernel, in_specs=lead + [pl.BlockSpec(memory_space=pltpu.V...  9.98 us
    all_to_all x1, waiting for transfers between devices, per_device(): sums = lax.all_to_all(parts, 'batch', 0, 0, tiled=True)  9.04 us
    ppermute x2, starting transfers between devices, swap(): return lax.ppermute(x, 'batch', [(i, i ^ 1) for i in range(shares)])  8.52 us
    pallas_call x1, Pallas kernels, per_device(): pl.pallas_call(send_kernel, grid=(channels // CHUNK,), in_specs=[sliced(i...  4.02 us
    all_to_all x1, waiting for transfers between devices, per_device(): lax.all_to_all(send, ('seq', 'batch'), 0, 0, tiled=True, axis_index_group...  2.36 us
  transfers between devices with their start and end apart: 4, of which 3 were waited for; matrix products, arithmetic and copies ran while one was open for 0% of the time, Pallas kernels for 8%

profile of v5, /device:TPU:1, one launch (start us, length us, event | category | flops | bytes accessed | tf_op | source)
XLA Modules:
  0.0 98.6 jit_solution(501020300937064164)
XLA Ops:
  0.6 4.0 %send.1 = bf16[64,32,512]{2,1,0:T(8,128)(2,1)} custom-call(bf16[1,1024,512]{2,1,0:T(8,128)(2,1)} %inputs.3, bf16[1,1024,512]{2,1,0:T(8,128)(2,1)} %gates.3, bf16[1,1024,512]{2,1,0:T(8,128)(2,1)} %cotangent.3, bf16[4,256,256]{2,1,0:T(8,128)(2,1)} %factor.3, bf16[8,128,128]{2,1,0:T(8,128)(2,1)} %second.1), custom_call_target="tpu_custom_call" | custom-call | flops 402653184 | bytes 6291456 | tf_op jit(solution)/shard_map/send/pallas_call | solution.py:244
  4.6 11.6 %all-to-all-start = ((bf16[64,32,512]{2,1,0:T(8,128)(2,1)}), bf16[64,32,512]{2,1,0:T(8,128)(2,1)S(1)}, u32[]{:S(2)}, u32[]{:S(2)}) async-start(bf16[64,32,512]{2,1,0:T(8,128)(2,1)} %send.1), calls=%async_computation | async-start | bytes 4194304 | tf_op jit(solution)/shard_map/all_to_all | solution.py:255
  16.3 3.1 %share.1 = (bf16[1024,512]{1,0:T(8,128)(2,1)}, bf16[1024,512]{1,0:T(8,128)(2,1)}) custom-call(s32[1]{0:T(128)} %bitcast.side, bf16[1,1024,512]{2,1,0:T(8,128)(2,1)} %inputs.3, bf16[1,1024,512]{2,1,0:T(8,128)(2,1)} %gates.3, bf16[1,1024,512]{2,1,0:T(8,128)(2,1)} %cotangent.3), custom_call_target="tpu_custom_call" | custom-call | bytes 5242880 | tf_op jit(solution)/shard_map/share/pallas_call | solution.py:209
  19.4 3.3 %collective-permute-start = (bf16[1024,512]{1,0:T(8,128)(2,1)}, bf16[1024,512]{1,0:T(8,128)(2,1)S(1)}, u32[]{:S(2)}, u32[]{:S(2)}) collective-permute-start(bf16[1024,512]{1,0:T(8,128)(2,1)} %get-tuple-element.7), channel_id=1, source_target_pairs={{0,1},{1,0},{2,3},{3,2},{4,5},{5,4},{6,7},{7,6},{8,9},{9,8},{10,11... | collective-permute-start | bytes 3145736 | tf_op jit(solution)/shard_map/ppermute | solution.py:241
  22.7 41.2 %collective-permute-done.after.came = bf16[1024,512]{1,0:T(8,128)(2,1)S(1)} collective-permute-done((bf16[1024,512]{1,0:T(8,128)(2,1)}, bf16[1024,512]{1,0:T(8,128)(2,1)S(1)}, u32[]{:S(2)}, u32[]{:S(2)}) %collective-permute-start) | collective-permute-done | bytes 1048608 | tf_op jit(solution)/shard_map/ppermute | solution.py:241
  63.9 2.4 %all-to-all-done = bf16[64,32,512]{2,1,0:T(8,128)(2,1)S(1)} async-done(((bf16[64,32,512]{2,1,0:T(8,128)(2,1)}), bf16[64,32,512]{2,1,0:T(8,128)(2,1)S(1)}, u32[]{:S(2)}, u32[]{:S(2)}) %all-to-all-start) | async-done | bytes 2097184 | tf_op jit(solution)/shard_map/all_to_all | solution.py:255
  66.3 0.0 copy-start.1
  66.3 0.8 theirs.1.after
  67.1 5.2 %collective-permute-start.1 = (bf16[32,16,512]{2,1,0:T(8,128)(2,1)}, bf16[32,16,512]{2,1,0:T(8,128)(2,1)}, u32[]{:S(2)}, u32[]{:S(2)}) collective-permute-start(bf16[32,16,512]{2,1,0:T(8,128)(2,1)} %theirs.1.after), channel_id=1, source_target_pairs={{0,1},{1,0},{2,3},{3,2},{4,5},{5,4},{6,7},{7,6},{8,9},{9,8},{10,11... | collective-permute-start | bytes 1572872 | tf_op jit(solution)/shard_map/ppermute | solution.py:241
  72.3 0.0 copy-done.1
  72.3 1.9 %grads.1 = bf16[16,48,256]{2,1,0:T(8,128)(2,1)} custom-call(s32[1]{0:T(128)} %bitcast.side, bf16[32,16,512]{2,1,0:T(8,128)(2,1)} %theirs.1.after, bf16[32,2,32,512]{3,2,1,0:T(8,128)(2,1)S(1)} %bitcast.3, bf16[1024,512]{1,0:T(8,128)(2,1)S(1)} %copy-done.1, bf16[1024,512]{1,0:T(8,128)(2,1)S(1)} %collective-permute-done.after.came), custom_call_target="tpu_custom_call" | custom-call | flops 402653184 | bytes 6291456 | tf_op jit(solution)/shard_map/grads/pallas_call | solution.py:209
  74.3 10.1 %all-to-all-start.1 = ((bf16[16,48,256]{2,1,0:T(8,128)(2,1)}), bf16[16,48,256]{2,1,0:T(8,128)(2,1)S(1)}, u32[]{:S(2)}, u32[]{:S(2)}) async-start(bf16[16,48,256]{2,1,0:T(8,128)(2,1)} %grads.1), calls=%async_computation.1 | async-start | bytes 786432 | tf_op jit(solution)/shard_map/all_to_all | solution.py:275
  84.4 0.0 copy-start
  84.4 1.0 %copy-done = bf16[4,256,256]{2,1,0:T(8,128)(2,1)S(1)} copy-done((bf16[4,256,256]{2,1,0:T(8,128)(2,1)S(1)}, bf16[4,256,256]{2,1,0:T(8,128)(2,1)}, u32[]{:S(2)}) %copy-start) | copy-done | bytes 524312
  85.5 1.1 %own.1.grad = bf16[1,1024,512]{2,1,0:T(8,128)(2,1)} custom-call(s32[1]{0:T(128)} %bitcast.side, bf16[32,2,32,512]{3,2,1,0:T(8,128)(2,1)S(1)} %bitcast.4, bf16[4,256,256]{2,1,0:T(8,128)(2,1)S(1)} %copy-done), custom_call_target="tpu_custom_call" | custom-call | flops 134217728 | bytes 2097152 | tf_op jit(solution)/shard_map/own/pallas_call | solution.py:209
  86.6 0.0 collective-permute-done.1.came
  86.6 2.2 %other.1 = bf16[1,1024,512]{2,1,0:T(8,128)(2,1)} custom-call(s32[1]{0:T(128)} %bitcast.side, bf16[32,16,512]{2,1,0:T(8,128)(2,1)} %collective-permute-done.1.came, bf16[4,256,256]{2,1,0:T(8,128)(2,1)S(1)} %copy-done, bf16[1,1024,512]{2,1,0:T(8,128)(2,1)} %own.1.grad), custom_call_target="tpu_custom_call", output_to_operand_aliasing={{}: (3, {})} | custom-call | flops 68719476736 | bytes 2097152 | tf_op jit(solution)/shard_map/other/pallas_call | solution.py:209
  88.8 9.0 %all-to-all-done.1.got = bf16[16,48,256]{2,1,0:T(8,128)(2,1)S(1)} async-done(((bf16[16,48,256]{2,1,0:T(8,128)(2,1)}), bf16[16,48,256]{2,1,0:T(8,128)(2,1)S(1)}, u32[]{:S(2)}, u32[]{:S(2)}) %all-to-all-start.1) | async-done | bytes 393248 | tf_op jit(solution)/shard_map/all_to_all | solution.py:275
  97.8 0.8 sums.1
Async XLA Ops:
  4.6 61.6 %all-to-all-start = ((bf16[64,32,512]{2,1,0:T(8,128)(2,1)}), bf16[64,32,512]{2,1,0:T(8,128)(2,1)S(1)}, u32[]{:S(2)}, u32[]{:S(2)}) async-start(bf16[64,32,512]{2,1,0:T(8,128)(2,1)} %send.1), calls=%async_computation | async-start | bytes 4194304 | tf_op jit(solution)/shard_map/all_to_all | solution.py:255
  19.4 44.5 %collective-permute-start = (bf16[1024,512]{1,0:T(8,128)(2,1)}, bf16[1024,512]{1,0:T(8,128)(2,1)S(1)}, u32[]{:S(2)}, u32[]{:S(2)}) collective-permute-start(bf16[1024,512]{1,0:T(8,128)(2,1)} %get-tuple-element.7), channel_id=1, source_target_pairs={{0,1},{1,0},{2,3},{3,2},{4,5},{5,4},{6,7},{7,6},{8,9},{9,8},{10,11... | collective-permute-start | bytes 3145736 | tf_op jit(solution)/shard_map/ppermute | solution.py:241
  66.3 6.1 %copy-start.1 = (bf16[1024,512]{1,0:T(8,128)(2,1)S(1)}, bf16[1024,512]{1,0:T(8,128)(2,1)}, u32[]{:S(2)}) copy-start(bf16[1024,512]{1,0:T(8,128)(2,1)} %get-tuple-element.8.own) | copy-start | bytes 3145732
  67.1 19.5 %collective-permute-start.1 = (bf16[32,16,512]{2,1,0:T(8,128)(2,1)}, bf16[32,16,512]{2,1,0:T(8,128)(2,1)}, u32[]{:S(2)}, u32[]{:S(2)}) collective-permute-start(bf16[32,16,512]{2,1,0:T(8,128)(2,1)} %theirs.1.after), channel_id=1, source_target_pairs={{0,1},{1,0},{2,3},{3,2},{4,5},{5,4},{6,7},{7,6},{8,9},{9,8},{10,11... | collective-permute-start | bytes 1572872 | tf_op jit(solution)/shard_map/ppermute | solution.py:241
  74.3 23.5 %all-to-all-start.1 = ((bf16[16,48,256]{2,1,0:T(8,128)(2,1)}), bf16[16,48,256]{2,1,0:T(8,128)(2,1)S(1)}, u32[]{:S(2)}, u32[]{:S(2)}) async-start(bf16[16,48,256]{2,1,0:T(8,128)(2,1)} %grads.1), calls=%async_computation.1 | async-start | bytes 786432 | tf_op jit(solution)/shard_map/all_to_all | solution.py:275
  84.4 1.0 %copy-start = (bf16[4,256,256]{2,1,0:T(8,128)(2,1)S(1)}, bf16[4,256,256]{2,1,0:T(8,128)(2,1)}, u32[]{:S(2)}) copy-start(bf16[4,256,256]{2,1,0:T(8,128)(2,1)} %factor.3) | copy-start | bytes 1572868
